TPU v7x, 32 devices: a whole 2x2x4 slice. The times are simulated.
32 devices in a mesh: sub: 8 (over z, x), crs: 4 (over y, core).
Axes of the slice: x: 2, y: 2, z: 4, core: 2. Of those that a mesh axis runs over, the one named last changes fastest.
Arguments:
- residual: float32 [32, 6, 3072], P('sub', None, 'crs'), may hold values from -6 to 6
- stiffness: float32 [32, 6, 3072], P('sub', None, 'crs'), may hold values from 0.1 to 10
- solid: int32 [32, 6, 16], P('sub', None, 'crs'), may hold values 0 or 1
- inverses: bfloat16 [32, 6, 192, 3072], P('sub', None, None, 'crs')
- coarse_basis: bfloat16 [32, 24, 6, 3072], P('sub', None, None, 'crs'), may hold values from -0.29882812 to 0.29882812
- assign: int32 [32], replicated, may hold values from 0 to 31, as said below
- corners: int32 [32, 8], P('sub'), may hold values from 0 to 31, as said below
- coarse_inverse: float32 [96, 96], P('crs')
Outputs:
- preconditioned: float32 [32, 6, 3072], P('sub', None, 'crs')
- inner_value: float32 [1], replicated
Inputs may be any that keep to these rules, and one draw needn't show every extreme that they name: assign is a permutation of the 32 subdomain numbers, set at run time by the load balancer, so a subdomain's neighbours may be held on any devices. corners[t, c] is the number of corner c = 4 cx + 2 cy + cz of subdomain assign[t], the grid vertex at its place plus (cx, cy, cz) taken periodically, under one fixed permutation of the 32 vertices.
All inputs are finite; a program needn't handle non-finite values. No bound on the sum of `solid` on one device may be relied on, other than what follows from the above.
Results may differ from a plain program's by a relative error of at most 0.0028.
Values sent between devices are 32-bit elements; how exact they have to be, the bound alone decides.
A program may use at most 128 MiB of HBM per device.

v0:
```python
import jax
import jax.numpy as jnp
from jax import lax
from jax.sharding import PartitionSpec as P


def partner_rows(assign, subs):
    depth = subs // 16
    slots = jnp.arange(subs, dtype=jnp.int32)
    inverse = jnp.sum(
        slots[:, None] * (assign[:, None] == slots[None, :]).astype(jnp.int32), axis=0
    )
    coord_a = assign // (4 * depth)
    coord_b = assign // depth % 4
    coord_c = assign % depth

    def number(first, second, third):
        return (first * 4 + second) * depth + third

    neighbours = jnp.stack(
        [
            number((coord_a + 1) % 4, coord_b, coord_c),
            number(coord_a, (coord_b + 1) % 4, coord_c),
            number(coord_a, coord_b, (coord_c + 1) % depth),
            number((coord_a + 3) % 4, coord_b, coord_c),
            number(coord_a, (coord_b + 3) % 4, coord_c),
            number(coord_a, coord_b, (coord_c + depth - 1) % depth),
        ],
        axis=1,
    )
    partner_slot = jnp.sum(
        inverse[None, None, :] * (neighbours[:, :, None] == slots[None, None, :]).astype(jnp.int32),
        axis=2,
    )
    partner_face = jnp.array([3, 4, 5, 0, 1, 2], dtype=jnp.int32)
    return (partner_slot * 6 + partner_face[None, :]).reshape(-1)


def body(residual, stiffness, solid, inverses, coarse_basis, assign, corners, coarse_inverse):
    slots_here, faces, width_here = residual.shape
    patches_here = solid.shape[2]
    entries = width_here // patches_here
    columns = lax.axis_size("crs")
    subs = assign.shape[0]
    face_rows = slots_here * faces
    rows = partner_rows(assign, subs)
    position = lax.axis_index("sub")
    own_rows = lax.dynamic_slice_in_dim(rows, position * face_rows, face_rows)
    flat_r = residual.reshape(face_rows, -1)
    flat_k = stiffness.reshape(face_rows, -1)
    solid_f = jnp.repeat(solid.astype(jnp.float32), entries, axis=2)
    all_r, all_k = (
        lax.all_gather(flat_r, "sub", axis=0, tiled=True),
        lax.all_gather(flat_k, "sub", axis=0, tiled=True),
    )
    partner_k = all_k[own_rows]
    weight = flat_k / (flat_k + partner_k)
    weight_partner = partner_k / (flat_k + partner_k)
    restricted_flat = weight * (flat_r + all_r[own_rows])
    restricted = (solid_f * restricted_flat.reshape(residual.shape)).astype(jnp.bfloat16)
    blocks = inverses.reshape(slots_here, faces, entries, patches_here, entries)
    vectors = restricted.reshape(slots_here, faces, patches_here, entries)
    local = jnp.einsum(
        "sfipj,sfpj->sfpi", blocks, vectors, preferred_element_type=jnp.float32
    ).reshape(residual.shape)
    coarse_part = jnp.einsum(
        "scfk,sfk->sc", coarse_basis, restricted, preferred_element_type=jnp.float32
    )
    total_coarse = 3 * subs
    index = (3 * corners[:, :, None] + jnp.arange(3, dtype=jnp.int32)[None, None, :]).reshape(
        slots_here, 24
    )
    onehot = (index[:, :, None] == jnp.arange(total_coarse, dtype=jnp.int32)[None, None, :]).astype(
        jnp.float32
    )
    coarse_local = jnp.einsum("sc,scn->n", coarse_part, onehot, precision=lax.Precision.HIGHEST)
    coarse_residual = lax.psum(coarse_local, ("sub", "crs"))
    block_width = total_coarse // columns
    start = lax.axis_index("crs") * block_width
    block_part = lax.dynamic_slice_in_dim(coarse_residual, start, block_width)
    terms = jnp.dot(block_part, coarse_inverse, precision=lax.Precision.HIGHEST)
    coarse_solution = lax.psum(terms, "crs")
    corner_values = jnp.einsum(
        "scn,n->sc", onehot, coarse_solution, precision=lax.Precision.HIGHEST
    ).astype(jnp.bfloat16)
    correction = jnp.einsum(
        "sc,scfk->sfk", corner_values, coarse_basis, preferred_element_type=jnp.float32
    )
    solution = solid_f * (local + correction)
    flat_u = solution.reshape(face_rows, -1)
    all_u = lax.all_gather(flat_u, "sub", axis=0, tiled=True)
    averaged = weight * flat_u + weight_partner * all_u[own_rows]
    preconditioned = averaged.reshape(residual.shape)
    inner_value = lax.psum(jnp.sum(residual * preconditioned), ("sub", "crs")).reshape(1)
    return (preconditioned, inner_value)


def solution(mesh):
    return jax.shard_map(
        body,
        mesh=mesh,
        in_specs=(
            P("sub", None, "crs"),
            P("sub", None, "crs"),
            P("sub", None, "crs"),
            P("sub", None, None, "crs"),
            P("sub", None, None, "crs"),
            P(),
            P("sub", None),
            P("crs", None),
        ),
        out_specs=(P("sub", None, "crs"), P()),
        check_vma=False,
    )
```

profile of v0, /device:TPU:0, one launch (start us, length us, event | category | flops | bytes accessed | tf_op | source)
XLA Modules:
  0.0 208.5 jit_solution(4053443274562115695)
XLA Ops:
  0.6 0.8 add_bitcast_fusion
  1.5 0.7 select_reduce_fusion.1
  2.2 0.3 select_reduce_fusion
  2.5 0.7 multiply_add_fusion
  3.5 0.9 copy.45
  4.4 33.2 %all_gather.9 = f32[192,768]{1,0:T(8,128)S(1)} all-gather(f32[24,768]{1,0:T(8,128)S(1)} %reshape.60), channel_id=1, replica_groups=mesh['sub'=8,'crs'=4] {'sub'}, dimensions={0}, use_global_device_ids=true | all-gather | bytes 663552 | tf_op jit(solution)/shard_map/all_gather | solution.py:54
  37.6 0.6 gather_fusion
  38.2 0.9 copy.48
  39.2 31.4 %all_gather.10 = f32[192,768]{1,0:T(8,128)S(1)} all-gather(f32[24,768]{1,0:T(8,128)S(1)} %reshape.62), channel_id=1, replica_groups=mesh['sub'=8,'crs'=4] {'sub'}, dimensions={0}, use_global_device_ids=true | all-gather | bytes 663552 | tf_op jit(solution)/shard_map/all_gather | solution.py:53
  70.6 0.6 gather_fusion.1
  71.2 0.7 convert_element_type.12
  72.2 1.0 fusion
  73.3 11.4 %copy.64 = bf16[4,6,192,768]{2,3,1,0:T(8,128)(2,1)} copy(bf16[4,6,192,768]{3,2,1,0:T(8,128)(2,1)} %param.12) | data formatting | bytes 14155776 | tf_op jit(solution)/shard_map/reshape | solution.py:61
  84.7 5.1 %fusion.27 = f32[4,6,4,1,192]{4,3,2,1,0:T(1,128)S(1)} fusion(bf16[4,6,4,192,1]{3,4,2,1,0:T(2,128)(2,1)S(1)} %reshape.108, bf16[4,6,192,4,192]{2,4,3,1,0:T(8,128)(2,1)} %bitcast.52), kind=kOutput, calls=%fused_computation.82 | convolution fusion | flops 7077888 | bytes 7188480 | tf_op jit(solution)/shard_map/sfipj,sfpj->sfpi/dot_general | solution.py:63
  89.9 0.4 convolution_bitcast_fusion
  90.8 39.8 %psum.21 = f32[96]{0:T(128)S(1)} all-reduce(f32[96]{0:T(128)S(1)} %convolution_bitcast_fusion.1), channel_id=1, replica_groups=mesh['sub'=8,'crs'=4] {'sub','crs'}, use_global_device_ids=true, to_apply=%region_2.3 | all-reduce | flops 96 | bytes 768 | tf_op jit(solution)/shard_map/psum | solution.py:77
  130.9 5.8 %psum.22 = f32[96]{0:T(128)S(1)} all-reduce(f32[96]{0:T(128)S(1)} %convolution_bitcast_fusion.2), channel_id=1, replica_groups=mesh['sub'=8,'crs'=4] {'crs'}, use_global_device_ids=true, to_apply=%region_3.4 | all-reduce | flops 96 | bytes 768 | tf_op jit(solution)/shard_map/psum | solution.py:82
  136.7 0.3 fusion.4
  137.0 0.3 fusion.7
  137.3 31.7 %all_gather.11 = f32[192,768]{1,0:T(8,128)S(1)} all-gather(f32[24,768]{1,0:T(8,128)S(1)} %reshape.66), channel_id=1, replica_groups=mesh['sub'=8,'crs'=4] {'sub'}, dimensions={0}, use_global_device_ids=true | all-gather | bytes 663552 | tf_op jit(solution)/shard_map/all_gather | solution.py:91
  169.1 0.6 gather_fusion.2
  169.7 0.7 multiply_reduce_fusion
  170.4 0.7 copy.54
  171.0 37.5 %psum.23 = f32[1]{0:T(128)} all-reduce(f32[1]{0:T(128)} %bitcast.20), channel_id=1, replica_groups=mesh['sub'=8,'crs'=4] {'sub','crs'}, use_global_device_ids=true, to_apply=%region_5.6 | all-reduce | flops 1 | bytes 8 | tf_op jit(solution)/shard_map/psum | solution.py:94
  (38 shorter events, 1.7 us)
Async XLA Ops:
  0.6 89.3 %copy-start = (bf16[4,24,6,768]{3,1,2,0:T(8,128)(2,1)S(1)}, bf16[4,24,6,768]{3,1,2,0:T(8,128)(2,1)}, u32[]{:S(2)}) copy-start(bf16[4,24,6,768]{3,1,2,0:T(8,128)(2,1)} %param.13) | copy-start | bytes 2654212
  84.7 5.7 %copy-start.4 = (s32[4,8]{1,0:T(4,128)S(1)}, s32[4,8]{1,0:T(4,128)}, u32[]{:S(2)}) copy-start(s32[4,8]{1,0:T(4,128)} %param.15) | copy-start | bytes 388
  84.7 46.0 %copy-start.3 = (f32[24,96]{1,0:T(8,128)S(1)}, f32[24,96]{1,0:T(8,128)}, u32[]{:S(2)}) copy-start(f32[24,96]{1,0:T(8,128)} %param.16) | copy-start | bytes 27652
  84.7 85.0 %copy-start.1 = (f32[4,6,768]{2,0,1:T(4,128)S(1)}, f32[4,6,768]{2,0,1:T(4,128)}, u32[]{:S(2)}) copy-start(f32[4,6,768]{2,0,1:T(4,128)} %param.9) | copy-start | bytes 221188
  84.7 85.0 %copy-start.2 = (f32[4,6,768]{2,0,1:T(4,128)S(1)}, f32[4,6,768]{2,0,1:T(4,128)}, u32[]{:S(2)}) copy-start(f32[4,6,768]{2,0,1:T(4,128)} %param.10) | copy-start | bytes 221188
where the time goes:
time: 210 us; the launch traced here: 208 us
  blocking collectives  179 us (85%)
  local copies, waits for them, and re-layouts  16.8 us (8%)
  matrix products  6.47 us (3%)
  other arithmetic  4.99 us (2%)
    psum x1, blocking collectives, body(): coarse_residual = lax.psum(coarse_local, ('sub', 'crs'))  39.8 us
    psum x1, blocking collectives, body(): lax.psum(jnp.sum(residual * preconditioned), ('sub', 'crs')).reshape(1)  37.5 us
    all_gather x1, blocking collectives, body(): lax.all_gather(flat_k, 'sub', axis=0, tiled=True)  33.2 us
    all_gather x1, blocking collectives, body(): all_u = lax.all_gather(flat_u, 'sub', axis=0, tiled=True)  31.7 us
    all_gather x1, blocking collectives, body(): lax.all_gather(flat_r, 'sub', axis=0, tiled=True)  31.4 us
    reshape x1, local copies, waits for them, and re-layouts, body(): blocks = inverses.reshape(slots_here, faces, entries, patches_here, entries)  11.4 us
    psum x1, blocking collectives, body(): coarse_solution = lax.psum(terms, 'crs')  5.8 us
    dot_general x1, matrix products, body(): jnp.einsum('sfipj,sfpj->sfpi', blocks, vectors, preferred_element_type=jn...  5.06 us

commit v1 on v0

v1 whole, which is shorter than its diff:
```python
import functools

import jax
import jax.numpy as jnp
from jax import lax
from jax.experimental import pallas as pl
from jax.experimental.pallas import tpu as pltpu
from jax.sharding import PartitionSpec as P

F32 = jnp.float32
BF16 = jnp.bfloat16
LANES = 128


def iota(shape, dim):
    return lax.broadcasted_iota(jnp.int32, shape, dim)


def split2(x):
    high = x.astype(BF16)
    low = (x - high.astype(F32)).astype(BF16)
    return high, low


def kernel(
    cfg,
    r_ref, k_ref, solid_ref, inv_hbm, basis_hbm, assign_ref, corners_ref, ci_ref,
    out_ref, inner_ref,
    inv, basis, s1, rb1, rx1, wts, tb2, tx2, b2, s3, rb3, rx3, tb4, tx4, b4,
    perm, smf, sm, xf, loc, corr, vt, sel, onehot, cv, ci,
    ca_s, ca_r, cb_s, cb_r, ia_s, ia_r, ib_s, ib_r,
    send, recv, own, load, small_send, small_recv, ci_send, ci_recv,
):
    n, m, slots, tiles, patches, entries, subs = cfg
    depth = subs // 16
    units = 3 * tiles
    base = units // n
    extra_any = units % n != 0
    rows_unit = 2 * slots
    rows_all = n * rows_unit
    rows_here = 6 * slots
    width = tiles * LANES
    nprim = basis.shape[1]
    coarse = ci_ref.shape[1]
    me = lax.axis_index("sub")
    mc = lax.axis_index("crs")

    def first(p):
        return (p * units + n - 1) // n

    def has_extra(p):
        return first(p + 1) - first(p) > base

    def row_of(l, f):
        return (f % 3) * rows_unit + (f // 3) * slots + l

    inv_load = [pltpu.make_async_copy(inv_hbm.at[l], inv.at[l], load.at[l]) for l in range(slots)]
    basis_load = pltpu.make_async_copy(basis_hbm, basis, load.at[slots])
    basis_load.start()
    for c in inv_load:
        c.start()

    def each_sub(body):
        if n <= 8:
            for k in range(1, n):
                body(k, lax.rem(me + k, n))
        else:
            def step(k, carry):
                body(k, lax.rem(me + k, n))
                return carry
            lax.fori_loop(1, n, step, 0)

    barrier = pltpu.get_barrier_semaphore()

    def greet(k, p):
        pl.semaphore_signal(barrier, inc=1, device_id={"sub": p}, device_id_type=pl.DeviceIdType.MESH)

    each_sub(greet)
    for k in range(1, m):
        pl.semaphore_signal(barrier, inc=1, device_id={"crs": lax.rem(mc + k, m)}, device_id_type=pl.DeviceIdType.MESH)

    for a, ref in enumerate((r_ref, k_ref)):
        for l in range(slots):
            for f in range(6):
                for ct in range(tiles):
                    row = (f // 3) * slots + l
                    s1[(f % 3) * tiles + ct, a, row:row + 1, :] = ref[l, f:f + 1, ct * LANES:(ct + 1) * LANES]

    def to_sub(src, dst, stage, kind, k, p):
        return pltpu.make_async_remote_copy(
            src_ref=src, dst_ref=dst, send_sem=send.at[stage, kind, k], recv_sem=recv.at[stage, kind, me],
            device_id={"sub": p}, device_id_type=pl.DeviceIdType.MESH)

    def from_sub(dst, stage, kind, p):
        pltpu.make_async_remote_copy(
            src_ref=dst, dst_ref=dst, send_sem=send.at[stage, kind, 0], recv_sem=recv.at[stage, kind, p],
            device_id={"sub": p}, device_id_type=pl.DeviceIdType.MESH).wait_recv()

    def spread(src, dst_base, dst_extra, stage):
        def go(k, p):
            if base:
                to_sub(src.at[pl.ds(first(p), base)], dst_base.at[me], stage, 0, k, p).start()
            if extra_any:
                @pl.when(has_extra(p))
                def _():
                    to_sub(src.at[first(p) + base], dst_extra.at[me], stage, 1, k, p).start()
        each_sub(go)
        if base:
            pltpu.make_async_copy(src.at[pl.ds(first(me), base)], dst_base.at[me], own.at[stage, 0]).start()
        if extra_any:
            @pl.when(has_extra(me))
            def _():
                pltpu.make_async_copy(src.at[first(me) + base], dst_extra.at[me], own.at[stage, 1]).start()

    def spread_wait(src, dst_base, dst_extra, stage):
        if base:
            pltpu.make_async_copy(src.at[pl.ds(first(me), base)], dst_base.at[me], own.at[stage, 0]).wait()
            each_sub(lambda k, p: from_sub(dst_base.at[p], stage, 0, p))
        if extra_any:
            @pl.when(has_extra(me))
            def _():
                pltpu.make_async_copy(src.at[first(me) + base], dst_extra.at[me], own.at[stage, 1]).wait()
                each_sub(lambda k, p: from_sub(dst_extra.at[p], stage, 1, p))

    def spread_done(src, dst_base, dst_extra, stage):
        def go(k, p):
            if base:
                to_sub(src.at[pl.ds(first(p), base)], dst_base.at[me], stage, 0, k, p).wait_send()
            if extra_any:
                @pl.when(has_extra(p))
                def _():
                    to_sub(src.at[first(p) + base], dst_extra.at[me], stage, 1, k, p).wait_send()
        each_sub(go)

    def back(src_base, src_extra, dst, stage):
        def go(k, p):
            if base:
                to_sub(src_base.at[p], dst.at[pl.ds(first(me), base)], stage, 0, k, p).start()
        each_sub(go)
        if base:
            pltpu.make_async_copy(src_base.at[me], dst.at[pl.ds(first(me), base)], own.at[stage, 0]).start()
        if extra_any:
            @pl.when(has_extra(me))
            def _():
                each_sub(lambda k, p: to_sub(src_extra.at[p], dst.at[first(me) + base], stage, 1, k, p).start())
                pltpu.make_async_copy(src_extra.at[me], dst.at[first(me) + base], own.at[stage, 1]).start()

    def back_wait(src_base, src_extra, dst, stage):
        if base:
            pltpu.make_async_copy(src_base.at[me], dst.at[pl.ds(first(me), base)], own.at[stage, 0]).wait()
        if extra_any:
            @pl.when(has_extra(me))
            def _():
                pltpu.make_async_copy(src_extra.at[me], dst.at[first(me) + base], own.at[stage, 1]).wait()

        def go(k, p):
            if base:
                from_sub(dst.at[pl.ds(first(p), base)], stage, 0, p)
            if extra_any:
                @pl.when(has_extra(p))
                def _():
                    from_sub(dst.at[first(p) + base], stage, 1, p)
        each_sub(go)

    def back_done(src_base, src_extra, dst, stage):
        if base:
            each_sub(lambda k, p: to_sub(src_base.at[p], dst.at[pl.ds(first(me), base)], stage, 0, k, p).wait_send())
        if extra_any:
            @pl.when(has_extra(me))
            def _():
                each_sub(lambda k, p: to_sub(src_extra.at[p], dst.at[first(me) + base], stage, 1, k, p).wait_send())

    def small_sub(src, dst, which, k, p):
        return pltpu.make_async_remote_copy(
            src_ref=src, dst_ref=dst.at[me], send_sem=small_send.at[which, k], recv_sem=small_recv.at[which, me],
            device_id={"sub": p}, device_id_type=pl.DeviceIdType.MESH)

    def small_sub_wait(dst, which, p):
        pltpu.make_async_remote_copy(
            src_ref=dst.at[p], dst_ref=dst.at[p], send_sem=small_send.at[which, 0], recv_sem=small_recv.at[which, p],
            device_id={"sub": p}, device_id_type=pl.DeviceIdType.MESH).wait_recv()

    def small_crs(src, dst, send_sem, recv_sem, k):
        return pltpu.make_async_remote_copy(
            src_ref=src, dst_ref=dst.at[mc], send_sem=send_sem.at[k], recv_sem=recv_sem.at[mc],
            device_id={"crs": lax.rem(mc + k, m)}, device_id_type=pl.DeviceIdType.MESH)

    def small_crs_wait(dst, send_sem, recv_sem, k):
        q = lax.rem(mc + k, m)
        pltpu.make_async_remote_copy(
            src_ref=dst.at[q], dst_ref=dst.at[q], send_sem=send_sem.at[0], recv_sem=recv_sem.at[q],
            device_id={"crs": q}, device_id_type=pl.DeviceIdType.MESH).wait_recv()

    pl.semaphore_wait(barrier, n - 1 + m - 1)
    spread(s1, rb1, rx1, 0)
    for k in range(1, m):
        small_crs(ci_ref, ci, ci_send, ci_recv, k).start()

    ci[mc] = ci_ref[...]
    assign_row = assign_ref[...]
    pick = iota((subs, subs), 0) == iota((subs, subs), 1)
    assign_col = jnp.sum(jnp.where(pick, assign_row, 0), axis=1, keepdims=True)
    slot_col = iota((rows_all, subs), 0) // rows_unit * slots + iota((rows_all, subs), 0) % slots
    a_col = jnp.sum(jnp.where(slot_col == iota((rows_all, subs), 1), assign_row, 0), axis=1, keepdims=True)
    slot_row = iota((subs, rows_all), 1) // rows_unit * slots + iota((subs, rows_all), 1) % slots
    a_row = jnp.sum(jnp.where(slot_row == iota((subs, rows_all), 0), assign_col, 0), axis=0, keepdims=True)
    side_col = iota((rows_all, rows_all), 0) // slots % 2
    side_row = iota((rows_all, rows_all), 1) // slots % 2

    def plus(a, d):
        step = (4 * depth, depth, 1)[d]
        size = (4, 4, depth)[d]
        place = (a // step) % size
        return a + jnp.where(place == size - 1, step * (1 - size), step)

    for d in range(3):
        ahead = (plus(a_col, d) == a_row) & (side_col == 0) & (side_row == 1)
        behind = (a_col == plus(a_row, d)) & (side_col == 1) & (side_row == 0)
        perm[d] = jnp.where(ahead | behind, 1.0, 0.0).astype(BF16)

    lane_patch = iota((6, width), 1) // entries
    for l in range(slots):
        flags = solid_ref[l].astype(F32)
        mask = jnp.zeros((6, width), F32)
        for p in range(patches):
            mask = jnp.where(lane_patch == p, flags[:, p:p + 1], mask)
        smf[l] = mask
    for l in range(slots):
        for f in range(6):
            sm[row_of(l, f):row_of(l, f) + 1, :] = smf[l, f:f + 1, :]

    total = slots * nprim
    part_row = iota((total, coarse), 0)
    index = jnp.zeros((total, coarse), jnp.int32)
    for l in range(slots):
        for c in range(nprim // 3):
            index = jnp.where(part_row // 3 == l * (nprim // 3) + c, 3 * corners_ref[l, c], index)
    index = index + part_row % 3
    onehot[...] = jnp.where(index == iota((total, coarse), 1), 1.0, 0.0).astype(F32)

    def restrict(u, j, r, k):
        p = perm[u // tiles]
        rh, rl = split2(r)
        kh, kl = split2(k)
        moved = jnp.dot(p, jnp.concatenate([rh, rl, kh, kl], axis=1), preferred_element_type=F32)
        rp = moved[:, :LANES] + moved[:, LANES:2 * LANES]
        kp = moved[:, 2 * LANES:3 * LANES] + moved[:, 3 * LANES:]
        scale = 1.0 / (k + kp)
        w = k * scale
        wts[j, 0] = w
        wts[j, 1] = kp * scale
        return (w * (r + rp)).reshape(n, rows_unit, LANES)

    spread_wait(s1, rb1, rx1, 0)
    for j in range(base):
        tb2[:, j] = restrict(
            first(me) + j, j, rb1[:, j, 0].reshape(rows_all, LANES), rb1[:, j, 1].reshape(rows_all, LANES))
    if extra_any:
        @pl.when(has_extra(me))
        def _():
            tx2[...] = restrict(
                first(me) + base, base, rx1[:, 0].reshape(rows_all, LANES), rx1[:, 1].reshape(rows_all, LANES))
    back(tb2, tx2, b2, 1)
    basis_load.wait()
    back_wait(tb2, tx2, b2, 1)

    lane_group = iota((rows_unit, LANES), 1)
    for d in range(3):
        for ct in range(tiles):
            lanes = slice(ct * LANES, (ct + 1) * LANES)
            group = slice(d * rows_unit, (d + 1) * rows_unit)
            value = (sm[group, lanes] * b2[d * tiles + ct]).astype(BF16).astype(F32)
            for p in range(patches):
                keep = (lane_group + ct * LANES) // entries == p
                vt[p * rows_here + d * rows_unit:p * rows_here + (d + 1) * rows_unit, lanes] = jnp.where(keep, value, 0.0)
            for side in range(2):
                for l in range(slots):
                    xf[l, d + 3 * side:d + 3 * side + 1, lanes] = value[side * slots + l:side * slots + l + 1]

    parts = []
    for l in range(slots):
        acc = jnp.zeros((nprim, 6, LANES), F32)
        for ct in range(tiles):
            lanes = slice(ct * LANES, (ct + 1) * LANES)
            acc = acc + basis[l, :, :, lanes].astype(F32) * xf[l, :, lanes][None]
        parts.append(jnp.sum(acc, axis=1))
    part = jnp.sum(jnp.concatenate(parts, axis=0), axis=1, keepdims=True)
    ca_s[...] = jnp.sum(part * onehot[...], axis=0, keepdims=True)
    ca_r[me] = ca_s[...]
    each_sub(lambda k, p: small_sub(ca_s, ca_r, 0, k, p).start())

    vectors = vt[...].astype(BF16)
    columns = vectors.shape[0]
    sel[...] = jnp.zeros_like(sel)
    col_row = iota((entries, columns), 1) % rows_here

    def solve(l):
        inv_load[l].wait()
        result = lax.dot_general(
            inv[l].reshape(6 * entries, width), vectors, (((1,), (1,)), ((), ())), preferred_element_type=F32)
        total_sel = sel[0:entries, 0:columns]
        for f in range(6):
            total_sel = jnp.where(col_row == row_of(l, f), result[f * entries:(f + 1) * entries], total_sel)
        sel[0:entries, 0:columns] = total_sel

    half = (slots + 1) // 2
    for l in range(half):
        solve(l)
    each_sub(lambda k, p: small_sub_wait(ca_r, 0, p))
    cb_s[...] = jnp.sum(ca_r[...], axis=0)
    cb_r[mc] = cb_s[...]
    for k in range(1, m):
        small_crs(cb_s, cb_r, small_send.at[2], small_recv.at[2], k).start()
    for l in range(half, slots):
        solve(l)
    turned = sel[...].T
    for p in range(patches):
        loc[:, p * entries:(p + 1) * entries] = turned[p * rows_here:(p + 1) * rows_here, :entries]

    for k in range(1, m):
        small_crs_wait(ci, ci_send, ci_recv, k)
    for k in range(1, m):
        small_crs_wait(cb_r, small_send.at[2], small_recv.at[2], k)
    residual_row = jnp.sum(cb_r[...], axis=0)
    diagonal = iota((coarse, coarse), 0) == iota((coarse, coarse), 1)
    residual_col = jnp.sum(jnp.where(diagonal, residual_row, 0.0), axis=1, keepdims=True)
    coarse_solution = jnp.sum(residual_col * ci[...].reshape(coarse, coarse), axis=0, keepdims=True)
    values = jnp.sum(onehot[...] * coarse_solution, axis=1, keepdims=True)
    cv[...] = jnp.broadcast_to(values.astype(BF16).astype(F32), cv.shape)
    for l in range(slots):
        for ct in range(tiles):
            lanes = slice(ct * LANES, (ct + 1) * LANES)
            acc = jnp.zeros((6, LANES), F32)
            for c in range(nprim):
                at = l * nprim + c
                acc = acc + basis[l, c, :, lanes].astype(F32) * cv[at:at + 1, :]
            for f in range(6):
                corr[row_of(l, f):row_of(l, f) + 1, lanes] = acc[f:f + 1]

    inner = jnp.zeros((rows_unit, LANES), F32)
    for d in range(3):
        for ct in range(tiles):
            lanes = slice(ct * LANES, (ct + 1) * LANES)
            group = slice(d * rows_unit, (d + 1) * rows_unit)
            u = sm[group, lanes] * (loc[group, lanes] + corr[group, lanes])
            s3[d * tiles + ct] = u
            inner = inner + u * b2[d * tiles + ct]
    spread(s3, rb3, rx3, 2)
    ia_s[...] = jnp.sum(inner, axis=0, keepdims=True)
    ia_r[me] = ia_s[...]
    each_sub(lambda k, p: small_sub(ia_s, ia_r, 1, k, p).start())

    def average(u, j, x):
        xh, xl = split2(x)
        moved = jnp.dot(perm[u // tiles], jnp.concatenate([xh, xl], axis=1), preferred_element_type=F32)
        xp = moved[:, :LANES] + moved[:, LANES:]
        return (wts[j, 0] * x + wts[j, 1] * xp).reshape(n, rows_unit, LANES)

    spread_wait(s3, rb3, rx3, 2)
    for j in range(base):
        tb4[:, j] = average(first(me) + j, j, rb3[:, j].reshape(rows_all, LANES))
    if extra_any:
        @pl.when(has_extra(me))
        def _():
            tx4[...] = average(first(me) + base, base, rx3[...].reshape(rows_all, LANES))
    back(tb4, tx4, b4, 3)
    each_sub(lambda k, p: small_sub_wait(ia_r, 1, p))
    ib_s[...] = jnp.sum(ia_r[...], axis=0)
    ib_r[mc] = ib_s[...]
    for k in range(1, m):
        small_crs(ib_s, ib_r, small_send.at[3], small_recv.at[3], k).start()

    spread_done(s1, rb1, rx1, 0)
    back_done(tb2, tx2, b2, 1)
    spread_done(s3, rb3, rx3, 2)
    for k in range(1, m):
        small_crs(ci_ref, ci, ci_send, ci_recv, k).wait_send()
        small_crs(cb_s, cb_r, small_send.at[2], small_recv.at[2], k).wait_send()
    each_sub(lambda k, p: small_sub(ca_s, ca_r, 0, k, p).wait_send())
    each_sub(lambda k, p: small_sub(ia_s, ia_r, 1, k, p).wait_send())

    back_wait(tb4, tx4, b4, 3)
    for l in range(slots):
        for f in range(6):
            for ct in range(tiles):
                row = (f // 3) * slots + l
                out_ref[l, f:f + 1, ct * LANES:(ct + 1) * LANES] = b4[(f % 3) * tiles + ct, row:row + 1, :]
    for k in range(1, m):
        small_crs_wait(ib_r, small_send.at[3], small_recv.at[3], k)
    inner_ref[...] = jnp.sum(jnp.sum(ib_r[...], axis=0), axis=1, keepdims=True)
    back_done(tb4, tx4, b4, 3)
    for k in range(1, m):
        small_crs(ib_s, ib_r, small_send.at[3], small_recv.at[3], k).wait_send()


def body(residual, stiffness, solid, inverses, coarse_basis, assign, corners, coarse_inverse):
    slots, faces, width = residual.shape
    patches = solid.shape[2]
    entries = width // patches
    n, m = lax.axis_size("sub"), lax.axis_size("crs")
    subs = assign.shape[0]
    tiles = width // LANES
    units = 3 * tiles
    base = units // n
    rows = 2 * slots
    rows_all = n * rows
    nprim = coarse_basis.shape[1]
    coarse = coarse_inverse.shape[1]
    cfg = (n, m, slots, tiles, patches, entries, subs)
    kept = max(base, 1)
    vt_rows = -(-(patches * rows * 3) // LANES) * LANES if patches * rows * 3 > LANES else patches * rows * 3
    square = -(-entries // LANES) * LANES
    lanes_sel = -(-vt_rows // LANES) * LANES
    vmem = pl.BlockSpec(memory_space=pltpu.VMEM)
    smem = pl.BlockSpec(memory_space=pltpu.SMEM)
    anyw = pl.BlockSpec(memory_space=pl.ANY)
    size = max(n, m)
    out, inner = pl.pallas_call(
        functools.partial(kernel, cfg),
        out_shape=(
            jax.ShapeDtypeStruct(residual.shape, F32),
            jax.ShapeDtypeStruct((1, 1), F32),
        ),
        in_specs=[vmem, vmem, vmem, anyw, anyw, vmem, smem, vmem],
        out_specs=(vmem, vmem),
        scratch_shapes=[
            pltpu.VMEM(inverses.shape, BF16),
            pltpu.VMEM(coarse_basis.shape, BF16),
            pltpu.VMEM((units, 2, rows, LANES), F32),
            pltpu.VMEM((n, kept, 2, rows, LANES), F32),
            pltpu.VMEM((n, 2, rows, LANES), F32),
            pltpu.VMEM((base + 1, 2, rows_all, LANES), F32),
            pltpu.VMEM((n, kept, rows, LANES), F32),
            pltpu.VMEM((n, rows, LANES), F32),
            pltpu.VMEM((units, rows, LANES), F32),
            pltpu.VMEM((units, rows, LANES), F32),
            pltpu.VMEM((n, kept, rows, LANES), F32),
            pltpu.VMEM((n, rows, LANES), F32),
            pltpu.VMEM((n, kept, rows, LANES), F32),
            pltpu.VMEM((n, rows, LANES), F32),
            pltpu.VMEM((units, rows, LANES), F32),
            pltpu.VMEM((3, rows_all, rows_all), BF16),
            pltpu.VMEM((slots, 6, width), F32),
            pltpu.VMEM((3 * rows, width), F32),
            pltpu.VMEM((slots, 6, width), F32),
            pltpu.VMEM((3 * rows, width), F32),
            pltpu.VMEM((3 * rows, width), F32),
            pltpu.VMEM((vt_rows, width), F32),
            pltpu.VMEM((square, lanes_sel), F32),
            pltpu.VMEM((slots * nprim, coarse), F32),
            pltpu.VMEM((slots * nprim, LANES), F32),
            pltpu.VMEM((m,) + coarse_inverse.shape, F32),
            pltpu.VMEM((1, coarse), F32),
            pltpu.VMEM((n, 1, coarse), F32),
            pltpu.VMEM((1, coarse), F32),
            pltpu.VMEM((m, 1, coarse), F32),
            pltpu.VMEM((1, LANES), F32),
            pltpu.VMEM((n, 1, LANES), F32),
            pltpu.VMEM((1, LANES), F32),
            pltpu.VMEM((m, 1, LANES), F32),
            pltpu.SemaphoreType.DMA((4, 2, n)),
            pltpu.SemaphoreType.DMA((4, 2, n)),
            pltpu.SemaphoreType.DMA((4, 2)),
            pltpu.SemaphoreType.DMA((slots + 1,)),
            pltpu.SemaphoreType.DMA((4, size)),
            pltpu.SemaphoreType.DMA((4, size)),
            pltpu.SemaphoreType.DMA((m,)),
            pltpu.SemaphoreType.DMA((m,)),
        ],
        compiler_params=pltpu.CompilerParams(
            collective_id=0, has_side_effects=True, vmem_limit_bytes=40 * 1024 * 1024
        ),
    )(residual, stiffness, solid, inverses, coarse_basis, assign.reshape(1, subs), corners, coarse_inverse)
    return out, inner.reshape(1)


def solution(mesh):
    return jax.shard_map(
        body,
        mesh=mesh,
        in_specs=(
            P("sub", None, "crs"),
            P("sub", None, "crs"),
            P("sub", None, "crs"),
            P("sub", None, None, "crs"),
            P("sub", None, None, "crs"),
            P(),
            P("sub", None),
            P("crs", None),
        ),
        out_specs=(P("sub", None, "crs"), P()),
        check_vma=False,
    )
```

time: 210 us -> 48.5 us (0.23)
  blocking collectives: 179 us -> 0 us
  Pallas kernels: 0 us -> 35.9 us
  local copies, waits for them, and re-layouts: 16.8 us -> 9.7 us
  matrix products: 6.47 us -> 0 us
  other arithmetic: 4.99 us -> 0 us
    all_gather x3 -> x0, blocking collectives: 96.3 us -> none  [the longest x1 33.2 us: body(): lax.all_gather(flat_k, 'sub', axis=0, tiled=True)]
    psum x3 -> x0, blocking collectives: 83.1 us -> none  [the longest x1 39.8 us: body(): coarse_residual = lax.psum(coarse_local, ('sub', 'crs'))]
    pallas_call x0 -> x1, Pallas kernels: none -> 35.9 us  [body(): pl.pallas_call(functools.partial(kernel, cfg), out_shape=(jax.ShapeDtypeS...]
    reshape x7 -> x0, local copies, waits for them, and re-layouts: 11.8 us -> none  [the longest x1 11.4 us: body(): blocks = inverses.reshape(slots_here, faces, entries, patches_here, entries)]
    unnamed x13, local copies, waits for them, and re-layouts: 2.5 us -> 9.7 us
    dot_general x6 -> x0, matrix products: 6.47 us -> none  [the longest x1 5.06 us: body(): jnp.einsum('sfipj,sfpj->sfpi', blocks, vectors, preferred_element_type=jn...]
where the time goes in v1:
time: 48.5 us; the launch traced here: 48 us
  Pallas kernels  35.9 us (74%)
  local copies, waits for them, and re-layouts  9.7 us (20%)
  between operations  2.41 us (5%)
    pallas_call x1, Pallas kernels, body(): pl.pallas_call(functools.partial(kernel, cfg), out_shape=(jax.ShapeDtypeS...  35.9 us
    unnamed x13, local copies, waits for them, and re-layouts  9.7 us

profile of v1, /device:TPU:0, one launch (start us, length us, event | category | flops | bytes accessed | tf_op | source)
XLA Modules:
  0.0 48.0 jit_solution(17404788891977838726)
XLA Ops:
  0.6 0.8 %copy.12.solid_ref = s32[4,6,4]{2,1,0:T(8,128)S(1)} copy(s32[4,6,4]{1,2,0:T(4,128)} %param.10) | data formatting | bytes 768 | tf_op args[2]
  1.4 0.9 %copy.10.r_ref = f32[4,6,768]{2,1,0:T(8,128)S(1)} copy(f32[4,6,768]{2,0,1:T(4,128)} %param.8) | data formatting | bytes 147456 | tf_op args[0]
  2.3 0.9 %copy.11.k_ref = f32[4,6,768]{2,1,0:T(8,128)S(1)} copy(f32[4,6,768]{2,0,1:T(4,128)} %param.9) | data formatting | bytes 147456 | tf_op args[1]
  3.2 1.4 %copy.13.basis_hbm = bf16[4,24,6,768]{3,2,1,0:T(8,128)(2,1)S(1)} copy(bf16[4,24,6,768]{3,1,2,0:T(8,128)(2,1)} %param.12) | data formatting | bytes 1769472 | tf_op args[4]
  4.6 0.0 copy-start
  4.6 3.0 %copy-done = bf16[4,6,192,768]{3,2,1,0:T(8,128)(2,1)S(1)} copy-done((bf16[4,6,192,768]{3,2,1,0:T(8,128)(2,1)S(1)}, bf16[4,6,192,768]{3,2,1,0:T(8,128)(2,1)}, u32[]{:S(2)}) %copy-start) | copy-done | bytes 7077912
  7.6 0.0 copy-start.1
  7.6 0.7 %copy-done.1 = f32[24,96]{1,0:T(8,128)S(1)} copy-done((f32[24,96]{1,0:T(8,128)S(1)}, f32[24,96]{1,0:T(8,128)}, u32[]{:S(2)}) %copy-start.1) | copy-done | bytes 9240
  8.4 0.0 copy-start.2
  8.4 0.7 %copy-done.2 = s32[4,8]{1,0:T(4,128)S(1)} copy-done((s32[4,8]{1,0:T(4,128)S(1)}, s32[4,8]{1,0:T(4,128)}, u32[]{:S(2)}) %copy-start.2) | copy-done | bytes 152
  9.0 0.0 copy-start.3
  9.0 0.7 %copy-done.3 = s32[32]{0:T(128)S(1)} copy-done((s32[32]{0:T(128)S(1)}, s32[32]{0:T(128)}, u32[]{:S(2)}) %copy-start.3) | copy-done | bytes 152
  9.7 35.9 %shard_map.95 = (f32[4,6,768]{2,1,0:T(8,128)S(1)}, f32[1,1]{1,0:T(1,128)}) custom-call(f32[4,6,768]{2,1,0:T(8,128)S(1)} %copy.10.r_ref, f32[4,6,768]{2,1,0:T(8,128)S(1)} %copy.11.k_ref, s32[4,6,4]{2,1,0:T(8,128)S(1)} %copy.12.solid_ref, bf16[4,6,192,768]{3,2,1,0:T(8,128)(2,1)S(1)} %copy-done, bf16[4,24,6,768]{3,2,1,0:T(8,128)(2,1)S(1)} %copy.13.basis_hbm, ...), custom_call_target="tpu_custom_call" | custom-call | tf_op jit(solution)/shard_map/pallas_call | solution.py:418
  45.6 0.7 %copy.14 = f32[4,6,768]{2,0,1:T(4,128)} copy(f32[4,6,768]{2,1,0:T(8,128)S(1)} %get-tuple-element.6) | data formatting | bytes 147456
Async XLA Ops:
  4.6 3.0 %copy-start = (bf16[4,6,192,768]{3,2,1,0:T(8,128)(2,1)S(1)}, bf16[4,6,192,768]{3,2,1,0:T(8,128)(2,1)}, u32[]{:S(2)}) copy-start(bf16[4,6,192,768]{3,2,1,0:T(8,128)(2,1)} %inv_hbm.1) | copy-start | bytes 21233668
  7.6 0.7 %copy-start.1 = (f32[24,96]{1,0:T(8,128)S(1)}, f32[24,96]{1,0:T(8,128)}, u32[]{:S(2)}) copy-start(f32[24,96]{1,0:T(8,128)} %ci_ref.1) | copy-start | bytes 27652
  8.4 0.7 %copy-start.2 = (s32[4,8]{1,0:T(4,128)S(1)}, s32[4,8]{1,0:T(4,128)}, u32[]{:S(2)}) copy-start(s32[4,8]{1,0:T(4,128)} %corners_ref.1) | copy-start | bytes 388
  9.0 0.7 %copy-start.3 = (s32[32]{0:T(128)S(1)}, s32[32]{0:T(128)}, u32[]{:S(2)}) copy-start(s32[32]{0:T(128)} %param.13) | copy-start | bytes 388

commit v2 on v1

--- a/solution.py
+++ b/solution.py
@@ -24,12 +24,13 @@
 
 def kernel(
     cfg,
-    r_ref, k_ref, solid_ref, inv_hbm, basis_hbm, assign_ref, corners_ref, ci_ref,
+    r_hbm, k_hbm, solid_hbm, inv_hbm, basis_hbm, assign_hbm, corners_hbm, ci_hbm,
     out_ref, inner_ref,
-    inv, basis, s1, rb1, rx1, wts, tb2, tx2, b2, s3, rb3, rx3, tb4, tx4, b4,
-    perm, smf, sm, xf, loc, corr, vt, sel, onehot, cv, ci,
+    r_ref, k_ref, solid_ref, assign_ref, corners_ref, ci_ref,
+    inv, basis, faces_basis, s1, rb1, rx1, wts, tb2, tx2, b2, s3, rb3, rx3, tb4, tx4, b4,
+    perm, sm, loc, corr, vt, vectors_ref, sel, onehot, onehot_t, ci, ci_t,
     ca_s, ca_r, cb_s, cb_r, ia_s, ia_r, ib_s, ib_r,
-    send, recv, own, load, small_send, small_recv, ci_send, ci_recv,
+    send, recv, own, load, small_load, small_send, small_recv, ci_send, ci_recv,
 ):
     n, m, slots, tiles, patches, entries, subs = cfg
     depth = subs // 16
@@ -40,7 +41,7 @@
     rows_all = n * rows_unit
     rows_here = 6 * slots
     width = tiles * LANES
-    nprim = basis.shape[1]
+    nprim = basis.shape[2]
     coarse = ci_ref.shape[1]
     me = lax.axis_index("sub")
     mc = lax.axis_index("crs")
@@ -54,9 +55,17 @@
     def row_of(l, f):
         return (f % 3) * rows_unit + (f // 3) * slots + l
 
-    inv_load = [pltpu.make_async_copy(inv_hbm.at[l], inv.at[l], load.at[l]) for l in range(slots)]
+    small = [
+        pltpu.make_async_copy(src, dst, small_load.at[i])
+        for i, (src, dst) in enumerate((
+            (r_hbm, r_ref), (k_hbm, k_ref), (ci_hbm, ci_ref), (assign_hbm, assign_ref),
+            (solid_hbm, solid_ref), (corners_hbm, corners_ref)))
+    ]
+    for c in small:
+        c.start()
     basis_load = pltpu.make_async_copy(basis_hbm, basis, load.at[slots])
     basis_load.start()
+    inv_load = [pltpu.make_async_copy(inv_hbm.at[l], inv.at[l], load.at[l]) for l in range(slots)]
     for c in inv_load:
         c.start()
 
@@ -80,11 +89,11 @@
         pl.semaphore_signal(barrier, inc=1, device_id={"crs": lax.rem(mc + k, m)}, device_id_type=pl.DeviceIdType.MESH)
 
     for a, ref in enumerate((r_ref, k_ref)):
-        for l in range(slots):
-            for f in range(6):
-                for ct in range(tiles):
-                    row = (f // 3) * slots + l
-                    s1[(f % 3) * tiles + ct, a, row:row + 1, :] = ref[l, f:f + 1, ct * LANES:(ct + 1) * LANES]
+        small[a].wait()
+        for f in range(6):
+            for ct in range(tiles):
+                row = (f // 3) * slots
+                s1[(f % 3) * tiles + ct, a, row:row + slots, :] = ref[f, :, ct * LANES:(ct + 1) * LANES]
 
     def to_sub(src, dst, stage, kind, k, p):
         return pltpu.make_async_remote_copy(
@@ -193,6 +202,8 @@
 
     pl.semaphore_wait(barrier, n - 1 + m - 1)
     spread(s1, rb1, rx1, 0)
+    for c in small[2:]:
+        c.wait()
     for k in range(1, m):
         small_crs(ci_ref, ci, ci_send, ci_recv, k).start()
 
@@ -200,12 +211,12 @@
     assign_row = assign_ref[...]
     pick = iota((subs, subs), 0) == iota((subs, subs), 1)
     assign_col = jnp.sum(jnp.where(pick, assign_row, 0), axis=1, keepdims=True)
-    slot_col = iota((rows_all, subs), 0) // rows_unit * slots + iota((rows_all, subs), 0) % slots
+    slot_col = iota((rows_all, 1), 0) // rows_unit * slots + iota((rows_all, 1), 0) % slots
     a_col = jnp.sum(jnp.where(slot_col == iota((rows_all, subs), 1), assign_row, 0), axis=1, keepdims=True)
-    slot_row = iota((subs, rows_all), 1) // rows_unit * slots + iota((subs, rows_all), 1) % slots
+    slot_row = iota((1, rows_all), 1) // rows_unit * slots + iota((1, rows_all), 1) % slots
     a_row = jnp.sum(jnp.where(slot_row == iota((subs, rows_all), 0), assign_col, 0), axis=0, keepdims=True)
-    side_col = iota((rows_all, rows_all), 0) // slots % 2
-    side_row = iota((rows_all, rows_all), 1) // slots % 2
+    side_col = iota((rows_all, 1), 0) // slots % 2
+    side_row = iota((1, rows_all), 1) // slots % 2
 
     def plus(a, d):
         step = (4 * depth, depth, 1)[d]
@@ -218,25 +229,41 @@
         behind = (a_col == plus(a_row, d)) & (side_col == 1) & (side_row == 0)
         perm[d] = jnp.where(ahead | behind, 1.0, 0.0).astype(BF16)
 
-    lane_patch = iota((6, width), 1) // entries
+    lane = iota((1, LANES), 1)
+    for p in range(patches):
+        flags = solid_ref[:, p, :].astype(F32)
+        for f in range(6):
+            flag = flags[:, f:f + 1]
+            at = row_of(0, f)
+            for ct in range(tiles):
+                low, high = p * entries - ct * LANES, (p + 1) * entries - ct * LANES
+                if low >= LANES or high <= 0:
+                    continue
+                lanes = slice(ct * LANES, (ct + 1) * LANES)
+                if low <= 0:
+                    sm[at:at + slots, lanes] = jnp.broadcast_to(flag, (slots, LANES))
+                else:
+                    sm[at:at + slots, lanes] = jnp.where(lane >= low, flag, sm[at:at + slots, lanes])
+
+    total = slots * nprim
+    ncorner = nprim // 3
+    part_col = iota((total, 1), 0)
+    group = part_col // 3
+    index = jnp.zeros((total, ncorner), jnp.int32)
     for l in range(slots):
-        flags = solid_ref[l].astype(F32)
-        mask = jnp.zeros((6, width), F32)
-        for p in range(patches):
-            mask = jnp.where(lane_patch == p, flags[:, p:p + 1], mask)
-        smf[l] = mask
-    for l in range(slots):
-        for f in range(6):
-            sm[row_of(l, f):row_of(l, f) + 1, :] = smf[l, f:f + 1, :]
-
-    total = slots * nprim
-    part_row = iota((total, coarse), 0)
-    index = jnp.zeros((total, coarse), jnp.int32)
-    for l in range(slots):
-        for c in range(nprim // 3):
-            index = jnp.where(part_row // 3 == l * (nprim // 3) + c, 3 * corners_ref[l, c], index)
-    index = index + part_row % 3
-    onehot[...] = jnp.where(index == iota((total, coarse), 1), 1.0, 0.0).astype(F32)
+        index = jnp.where(group == l * ncorner + iota((1, ncorner), 1), corners_ref[l:l + 1, :], index)
+    index = 3 * jnp.sum(index, axis=1, keepdims=True) + part_col % 3
+    hot = jnp.where(index == iota((total, coarse), 1), 1.0, 0.0).astype(F32)
+    onehot[...] = hot
+    onehot_t[...] = hot.T
+    vt[...] = jnp.zeros_like(vt)
+    col_row = iota((1, vt.shape[0]), 1) % rows_here
+    sel[...] = jnp.zeros_like(sel)
+
+    basis_load.wait()
+    for f in range(6):
+        faces_basis[f] = jnp.concatenate(
+            [basis[l, f].astype(F32) for l in range(slots)], axis=0).astype(BF16)
 
     def restrict(u, j, r, k):
         p = perm[u // tiles]
@@ -261,43 +288,49 @@
             tx2[...] = restrict(
                 first(me) + base, base, rx1[:, 0].reshape(rows_all, LANES), rx1[:, 1].reshape(rows_all, LANES))
     back(tb2, tx2, b2, 1)
-    basis_load.wait()
+    for k in range(1, m):
+        small_crs_wait(ci, ci_send, ci_recv, k)
+    ci_t[...] = ci[...].reshape(coarse, coarse).T
     back_wait(tb2, tx2, b2, 1)
 
-    lane_group = iota((rows_unit, LANES), 1)
     for d in range(3):
         for ct in range(tiles):
             lanes = slice(ct * LANES, (ct + 1) * LANES)
             group = slice(d * rows_unit, (d + 1) * rows_unit)
-            value = (sm[group, lanes] * b2[d * tiles + ct]).astype(BF16).astype(F32)
+            value = sm[group, lanes] * b2[d * tiles + ct]
             for p in range(patches):
-                keep = (lane_group + ct * LANES) // entries == p
-                vt[p * rows_here + d * rows_unit:p * rows_here + (d + 1) * rows_unit, lanes] = jnp.where(keep, value, 0.0)
-            for side in range(2):
-                for l in range(slots):
-                    xf[l, d + 3 * side:d + 3 * side + 1, lanes] = value[side * slots + l:side * slots + l + 1]
-
+                low, high = p * entries - ct * LANES, (p + 1) * entries - ct * LANES
+                if low >= LANES or high <= 0:
+                    continue
+                kept = value
+                if low > 0:
+                    kept = jnp.where(lane >= low, kept, 0.0)
+                if high < LANES:
+                    kept = jnp.where(lane < high, kept, 0.0)
+                at = p * rows_here + d * rows_unit
+                vt[at:at + rows_unit, lanes] = kept
+    for ct in range(tiles):
+        lanes = slice(ct * LANES, (ct + 1) * LANES)
+        vectors_ref[lanes, :] = vt[:, lanes].T.astype(BF16)
+    vectors = vectors_ref[...]
+    columns = vectors.shape[1]
+
+    products = jnp.dot(faces_basis[...].reshape(6 * total, width), vectors, preferred_element_type=F32)
     parts = []
     for l in range(slots):
-        acc = jnp.zeros((nprim, 6, LANES), F32)
-        for ct in range(tiles):
-            lanes = slice(ct * LANES, (ct + 1) * LANES)
-            acc = acc + basis[l, :, :, lanes].astype(F32) * xf[l, :, lanes][None]
-        parts.append(jnp.sum(acc, axis=1))
+        acc = jnp.zeros((nprim, columns), F32)
+        for f in range(6):
+            at = f * total + l * nprim
+            acc = jnp.where(col_row == row_of(l, f), products[at:at + nprim], 0.0) + acc
+        parts.append(acc)
     part = jnp.sum(jnp.concatenate(parts, axis=0), axis=1, keepdims=True)
     ca_s[...] = jnp.sum(part * onehot[...], axis=0, keepdims=True)
     ca_r[me] = ca_s[...]
     each_sub(lambda k, p: small_sub(ca_s, ca_r, 0, k, p).start())
 
-    vectors = vt[...].astype(BF16)
-    columns = vectors.shape[0]
-    sel[...] = jnp.zeros_like(sel)
-    col_row = iota((entries, columns), 1) % rows_here
-
     def solve(l):
         inv_load[l].wait()
-        result = lax.dot_general(
-            inv[l].reshape(6 * entries, width), vectors, (((1,), (1,)), ((), ())), preferred_element_type=F32)
+        result = jnp.dot(inv[l].reshape(6 * entries, width), vectors, preferred_element_type=F32)
         total_sel = sel[0:entries, 0:columns]
         for f in range(6):
             total_sel = jnp.where(col_row == row_of(l, f), result[f * entries:(f + 1) * entries], total_sel)
@@ -318,24 +351,19 @@
         loc[:, p * entries:(p + 1) * entries] = turned[p * rows_here:(p + 1) * rows_here, :entries]
 
     for k in range(1, m):
-        small_crs_wait(ci, ci_send, ci_recv, k)
-    for k in range(1, m):
         small_crs_wait(cb_r, small_send.at[2], small_recv.at[2], k)
     residual_row = jnp.sum(cb_r[...], axis=0)
-    diagonal = iota((coarse, coarse), 0) == iota((coarse, coarse), 1)
-    residual_col = jnp.sum(jnp.where(diagonal, residual_row, 0.0), axis=1, keepdims=True)
-    coarse_solution = jnp.sum(residual_col * ci[...].reshape(coarse, coarse), axis=0, keepdims=True)
-    values = jnp.sum(onehot[...] * coarse_solution, axis=1, keepdims=True)
-    cv[...] = jnp.broadcast_to(values.astype(BF16).astype(F32), cv.shape)
-    for l in range(slots):
-        for ct in range(tiles):
-            lanes = slice(ct * LANES, (ct + 1) * LANES)
-            acc = jnp.zeros((6, LANES), F32)
-            for c in range(nprim):
-                at = l * nprim + c
-                acc = acc + basis[l, c, :, lanes].astype(F32) * cv[at:at + 1, :]
-            for f in range(6):
-                corr[row_of(l, f):row_of(l, f) + 1, lanes] = acc[f:f + 1]
+    coarse_solution = jnp.sum(ci_t[...] * residual_row, axis=1, keepdims=True)
+    values = jnp.sum(onehot_t[...] * coarse_solution, axis=0, keepdims=True)
+    slot_at = iota((rows_unit, 1), 0) % slots * nprim
+    place = iota((1, total), 1)
+    corner_values = jnp.where((place >= slot_at) & (place < slot_at + nprim), values, 0.0).astype(BF16)
+    near = iota((rows_unit, 1), 0) < slots
+    for d in range(3):
+        corr[d * rows_unit:(d + 1) * rows_unit, :] = jnp.where(
+            near,
+            jnp.dot(corner_values, faces_basis[d], preferred_element_type=F32),
+            jnp.dot(corner_values, faces_basis[d + 3], preferred_element_type=F32))
 
     inner = jnp.zeros((rows_unit, LANES), F32)
     for d in range(3):
@@ -380,11 +408,10 @@
     each_sub(lambda k, p: small_sub(ia_s, ia_r, 1, k, p).wait_send())
 
     back_wait(tb4, tx4, b4, 3)
-    for l in range(slots):
-        for f in range(6):
-            for ct in range(tiles):
-                row = (f // 3) * slots + l
-                out_ref[l, f:f + 1, ct * LANES:(ct + 1) * LANES] = b4[(f % 3) * tiles + ct, row:row + 1, :]
+    for f in range(6):
+        for ct in range(tiles):
+            row = (f // 3) * slots
+            out_ref[f, :, ct * LANES:(ct + 1) * LANES] = b4[(f % 3) * tiles + ct, row:row + slots, :]
     for k in range(1, m):
         small_crs_wait(ib_r, small_send.at[3], small_recv.at[3], k)
     inner_ref[...] = jnp.sum(jnp.sum(ib_r[...], axis=0), axis=1, keepdims=True)
@@ -408,24 +435,29 @@
     coarse = coarse_inverse.shape[1]
     cfg = (n, m, slots, tiles, patches, entries, subs)
     kept = max(base, 1)
-    vt_rows = -(-(patches * rows * 3) // LANES) * LANES if patches * rows * 3 > LANES else patches * rows * 3
+    vt_rows = -(-(patches * rows * 3) // LANES) * LANES
     square = -(-entries // LANES) * LANES
-    lanes_sel = -(-vt_rows // LANES) * LANES
     vmem = pl.BlockSpec(memory_space=pltpu.VMEM)
-    smem = pl.BlockSpec(memory_space=pltpu.SMEM)
     anyw = pl.BlockSpec(memory_space=pl.ANY)
     size = max(n, m)
     out, inner = pl.pallas_call(
         functools.partial(kernel, cfg),
         out_shape=(
-            jax.ShapeDtypeStruct(residual.shape, F32),
+            jax.ShapeDtypeStruct((faces, slots, width), F32),
             jax.ShapeDtypeStruct((1, 1), F32),
         ),
-        in_specs=[vmem, vmem, vmem, anyw, anyw, vmem, smem, vmem],
+        in_specs=[anyw] * 8,
         out_specs=(vmem, vmem),
         scratch_shapes=[
+            pltpu.VMEM((faces, slots, width), F32),
+            pltpu.VMEM((faces, slots, width), F32),
+            pltpu.VMEM((slots, patches, faces), jnp.int32),
+            pltpu.VMEM((1, subs), jnp.int32),
+            pltpu.VMEM(corners.shape, jnp.int32),
+            pltpu.VMEM(coarse_inverse.shape, F32),
             pltpu.VMEM(inverses.shape, BF16),
-            pltpu.VMEM(coarse_basis.shape, BF16),
+            pltpu.VMEM((slots, faces, nprim, width), BF16),
+            pltpu.VMEM((faces, slots * nprim, width), BF16),
             pltpu.VMEM((units, 2, rows, LANES), F32),
             pltpu.VMEM((n, kept, 2, rows, LANES), F32),
             pltpu.VMEM((n, 2, rows, LANES), F32),
@@ -440,16 +472,16 @@
             pltpu.VMEM((n, rows, LANES), F32),
             pltpu.VMEM((units, rows, LANES), F32),
             pltpu.VMEM((3, rows_all, rows_all), BF16),
-            pltpu.VMEM((slots, 6, width), F32),
             pltpu.VMEM((3 * rows, width), F32),
-            pltpu.VMEM((slots, 6, width), F32),
             pltpu.VMEM((3 * rows, width), F32),
             pltpu.VMEM((3 * rows, width), F32),
             pltpu.VMEM((vt_rows, width), F32),
-            pltpu.VMEM((square, lanes_sel), F32),
+            pltpu.VMEM((width, vt_rows), BF16),
+            pltpu.VMEM((square, vt_rows), F32),
             pltpu.VMEM((slots * nprim, coarse), F32),
-            pltpu.VMEM((slots * nprim, LANES), F32),
+            pltpu.VMEM((coarse, slots * nprim), F32),
             pltpu.VMEM((m,) + coarse_inverse.shape, F32),
+            pltpu.VMEM((coarse, coarse), F32),
             pltpu.VMEM((1, coarse), F32),
             pltpu.VMEM((n, 1, coarse), F32),
             pltpu.VMEM((1, coarse), F32),
@@ -462,16 +494,19 @@
             pltpu.SemaphoreType.DMA((4, 2, n)),
             pltpu.SemaphoreType.DMA((4, 2)),
             pltpu.SemaphoreType.DMA((slots + 1,)),
+            pltpu.SemaphoreType.DMA((6,)),
             pltpu.SemaphoreType.DMA((4, size)),
             pltpu.SemaphoreType.DMA((4, size)),
             pltpu.SemaphoreType.DMA((m,)),
             pltpu.SemaphoreType.DMA((m,)),
         ],
         compiler_params=pltpu.CompilerParams(
-            collective_id=0, has_side_effects=True, vmem_limit_bytes=40 * 1024 * 1024
+            collective_id=0, has_side_effects=True, vmem_limit_bytes=60 * 1024 * 1024
         ),
-    )(residual, stiffness, solid, inverses, coarse_basis, assign.reshape(1, subs), corners, coarse_inverse)
-    return out, inner.reshape(1)
+    )(
+        residual.transpose(1, 0, 2), stiffness.transpose(1, 0, 2), solid.transpose(0, 2, 1), inverses,
+        coarse_basis.transpose(0, 2, 1, 3), assign.reshape(1, subs), corners, coarse_inverse)
+    return out.transpose(1, 0, 2), inner.reshape(1)
 
 
 def solution(mesh):

time: 48.5 us -> 38.2 us (0.79)
  local copies, waits for them, and re-layouts: 9.7 us -> 1.52 us
  Pallas kernels: 35.9 us -> 34.1 us
    unnamed x13 -> x1, local copies, waits for them, and re-layouts: 9.7 us -> 1.52 us
    pallas_call x1, Pallas kernels: 35.9 us -> 34.1 us  [body(): pl.pallas_call(functools.partial(kernel, cfg), out_shape=(jax.ShapeDtypeS...]
where the time goes in v2:
time: 38.2 us; the launch traced here: 38 us
  Pallas kernels  34.1 us (89%)
  between operations  2.33 us (6%)
  local copies, waits for them, and re-layouts  1.52 us (4%)
    pallas_call x1, Pallas kernels, body(): pl.pallas_call(functools.partial(kernel, cfg), out_shape=(jax.ShapeDtypeS...  34.1 us
    unnamed x1, local copies, waits for them, and re-layouts  1.52 us

profile of v2, /device:TPU:0, one launch (start us, length us, event | category | flops | bytes accessed | tf_op | source)
XLA Modules:
  0.0 38.0 jit_solution(3690709930847695428)
XLA Ops:
  0.6 34.1 %shard_map.95 = (f32[6,4,768]{2,1,0:T(4,128)}, f32[1,1]{1,0:T(1,128)}) custom-call(f32[6,4,768]{2,1,0:T(4,128)} %bitcast.9, f32[6,4,768]{2,1,0:T(4,128)} %bitcast.10, s32[4,4,6]{2,1,0:T(4,128)} %bitcast.11, bf16[4,6,192,768]{3,2,1,0:T(8,128)(2,1)} %inv_hbm.1, bf16[4,6,24,768]{3,2,1,0:T(8,128)(2,1)} %bitcast.7, s32[1,32]{1,0:T(1,128)} %bitcast.12, ...), custom_call_target="tpu_custom_call" | custom-call | tf_op jit(solution)/shard_map/pallas_call | solution.py:443
  34.8 1.5 %copy.12 = f32[4,6,768]{2,0,1:T(4,128)} copy(f32[4,6,768]{2,0,1:T(4,128)} %bitcast.8) | data formatting | bytes 147456

commit v3 on v2

--- a/solution.py
+++ b/solution.py
@@ -121,15 +121,14 @@
             def _():
                 pltpu.make_async_copy(src.at[first(me) + base], dst_extra.at[me], own.at[stage, 1]).start()
 
-    def spread_wait(src, dst_base, dst_extra, stage):
+    def spread_wait(src, dst_base, stage):
         if base:
             pltpu.make_async_copy(src.at[pl.ds(first(me), base)], dst_base.at[me], own.at[stage, 0]).wait()
             each_sub(lambda k, p: from_sub(dst_base.at[p], stage, 0, p))
-        if extra_any:
-            @pl.when(has_extra(me))
-            def _():
-                pltpu.make_async_copy(src.at[first(me) + base], dst_extra.at[me], own.at[stage, 1]).wait()
-                each_sub(lambda k, p: from_sub(dst_extra.at[p], stage, 1, p))
+
+    def spread_wait_extra(src, dst_extra, stage):
+        pltpu.make_async_copy(src.at[first(me) + base], dst_extra.at[me], own.at[stage, 1]).wait()
+        each_sub(lambda k, p: from_sub(dst_extra.at[p], stage, 1, p))
 
     def spread_done(src, dst_base, dst_extra, stage):
         def go(k, p):
@@ -141,16 +140,20 @@
                     to_sub(src.at[first(p) + base], dst_extra.at[me], stage, 1, k, p).wait_send()
         each_sub(go)
 
-    def back(src_base, src_extra, dst, stage):
+    def back(src_base, dst, stage):
         def go(k, p):
             if base:
                 to_sub(src_base.at[p], dst.at[pl.ds(first(me), base)], stage, 0, k, p).start()
         each_sub(go)
         if base:
             pltpu.make_async_copy(src_base.at[me], dst.at[pl.ds(first(me), base)], own.at[stage, 0]).start()
+
+    def back_extra(src_in, dst_in, src_extra, dst, stage, compute):
         if extra_any:
             @pl.when(has_extra(me))
             def _():
+                spread_wait_extra(src_in, dst_in, stage - 1)
+                src_extra[...] = compute()
                 each_sub(lambda k, p: to_sub(src_extra.at[p], dst.at[first(me) + base], stage, 1, k, p).start())
                 pltpu.make_async_copy(src_extra.at[me], dst.at[first(me) + base], own.at[stage, 1]).start()
 
@@ -278,16 +281,13 @@
         wts[j, 1] = kp * scale
         return (w * (r + rp)).reshape(n, rows_unit, LANES)
 
-    spread_wait(s1, rb1, rx1, 0)
+    spread_wait(s1, rb1, 0)
     for j in range(base):
         tb2[:, j] = restrict(
             first(me) + j, j, rb1[:, j, 0].reshape(rows_all, LANES), rb1[:, j, 1].reshape(rows_all, LANES))
-    if extra_any:
-        @pl.when(has_extra(me))
-        def _():
-            tx2[...] = restrict(
-                first(me) + base, base, rx1[:, 0].reshape(rows_all, LANES), rx1[:, 1].reshape(rows_all, LANES))
-    back(tb2, tx2, b2, 1)
+    back(tb2, b2, 1)
+    back_extra(s1, rx1, tx2, b2, 1, lambda: restrict(
+        first(me) + base, base, rx1[:, 0].reshape(rows_all, LANES), rx1[:, 1].reshape(rows_all, LANES)))
     for k in range(1, m):
         small_crs_wait(ci, ci_send, ci_recv, k)
     ci_t[...] = ci[...].reshape(coarse, coarse).T
@@ -384,14 +384,11 @@
         xp = moved[:, :LANES] + moved[:, LANES:]
         return (wts[j, 0] * x + wts[j, 1] * xp).reshape(n, rows_unit, LANES)
 
-    spread_wait(s3, rb3, rx3, 2)
+    spread_wait(s3, rb3, 2)
     for j in range(base):
         tb4[:, j] = average(first(me) + j, j, rb3[:, j].reshape(rows_all, LANES))
-    if extra_any:
-        @pl.when(has_extra(me))
-        def _():
-            tx4[...] = average(first(me) + base, base, rx3[...].reshape(rows_all, LANES))
-    back(tb4, tx4, b4, 3)
+    back(tb4, b4, 3)
+    back_extra(s3, rx3, tx4, b4, 3, lambda: average(first(me) + base, base, rx3[...].reshape(rows_all, LANES)))
     each_sub(lambda k, p: small_sub_wait(ia_r, 1, p))
     ib_s[...] = jnp.sum(ia_r[...], axis=0)
     ib_r[mc] = ib_s[...]

time: 38.2 us -> 37.9 us (level)
  no operation moved by 1% of the time
where the time goes in v3:
time: 37.9 us; the launch traced here: 37.7 us
  Pallas kernels  33.9 us (89%)
  between operations  2.33 us (6%)
  local copies, waits for them, and re-layouts  1.52 us (4%)
    pallas_call x1, Pallas kernels, body(): pl.pallas_call(functools.partial(kernel, cfg), out_shape=(jax.ShapeDtypeS...  33.9 us
    unnamed x1, local copies, waits for them, and re-layouts  1.52 us

profile of v3, /device:TPU:0, one launch (start us, length us, event | category | flops | bytes accessed | tf_op | source)
XLA Modules:
  0.0 37.7 jit_solution(12701977891037975776)
XLA Ops:
  0.6 33.9 %shard_map.95 = (f32[6,4,768]{2,1,0:T(4,128)}, f32[1,1]{1,0:T(1,128)}) custom-call(f32[6,4,768]{2,1,0:T(4,128)} %bitcast.9, f32[6,4,768]{2,1,0:T(4,128)} %bitcast.10, s32[4,4,6]{2,1,0:T(4,128)} %bitcast.11, bf16[4,6,192,768]{3,2,1,0:T(8,128)(2,1)} %inv_hbm.1, bf16[4,6,24,768]{3,2,1,0:T(8,128)(2,1)} %bitcast.7, s32[1,32]{1,0:T(1,128)} %bitcast.12, ...), custom_call_target="tpu_custom_call" | custom-call | tf_op jit(solution)/shard_map/pallas_call | solution.py:440
  34.5 1.5 %copy.12 = f32[4,6,768]{2,0,1:T(4,128)} copy(f32[4,6,768]{2,0,1:T(4,128)} %bitcast.8) | data formatting | bytes 147456

commit v4 on v3

--- a/solution.py
+++ b/solution.py
@@ -248,6 +248,26 @@
                 else:
                     sm[at:at + slots, lanes] = jnp.where(lane >= low, flag, sm[at:at + slots, lanes])
 
+    def restrict(u, j, r, k):
+        p = perm[u // tiles]
+        rh, rl = split2(r)
+        kh, kl = split2(k)
+        moved = jnp.dot(p, jnp.concatenate([rh, rl, kh, kl], axis=1), preferred_element_type=F32)
+        rp = moved[:, :LANES] + moved[:, LANES:2 * LANES]
+        kp = moved[:, 2 * LANES:3 * LANES] + moved[:, 3 * LANES:]
+        scale = 1.0 / (k + kp)
+        w = k * scale
+        wts[j, 0] = w
+        wts[j, 1] = kp * scale
+        return (w * (r + rp)).reshape(n, rows_unit, LANES)
+
+    spread_wait(s1, rb1, 0)
+    for j in range(base):
+        tb2[:, j] = restrict(
+            first(me) + j, j, rb1[:, j, 0].reshape(rows_all, LANES), rb1[:, j, 1].reshape(rows_all, LANES))
+    back(tb2, b2, 1)
+    back_extra(s1, rx1, tx2, b2, 1, lambda: restrict(
+        first(me) + base, base, rx1[:, 0].reshape(rows_all, LANES), rx1[:, 1].reshape(rows_all, LANES)))
     total = slots * nprim
     ncorner = nprim // 3
     part_col = iota((total, 1), 0)
@@ -268,26 +288,6 @@
         faces_basis[f] = jnp.concatenate(
             [basis[l, f].astype(F32) for l in range(slots)], axis=0).astype(BF16)
 
-    def restrict(u, j, r, k):
-        p = perm[u // tiles]
-        rh, rl = split2(r)
-        kh, kl = split2(k)
-        moved = jnp.dot(p, jnp.concatenate([rh, rl, kh, kl], axis=1), preferred_element_type=F32)
-        rp = moved[:, :LANES] + moved[:, LANES:2 * LANES]
-        kp = moved[:, 2 * LANES:3 * LANES] + moved[:, 3 * LANES:]
-        scale = 1.0 / (k + kp)
-        w = k * scale
-        wts[j, 0] = w
-        wts[j, 1] = kp * scale
-        return (w * (r + rp)).reshape(n, rows_unit, LANES)
-
-    spread_wait(s1, rb1, 0)
-    for j in range(base):
-        tb2[:, j] = restrict(
-            first(me) + j, j, rb1[:, j, 0].reshape(rows_all, LANES), rb1[:, j, 1].reshape(rows_all, LANES))
-    back(tb2, b2, 1)
-    back_extra(s1, rx1, tx2, b2, 1, lambda: restrict(
-        first(me) + base, base, rx1[:, 0].reshape(rows_all, LANES), rx1[:, 1].reshape(rows_all, LANES)))
     for k in range(1, m):
         small_crs_wait(ci, ci_send, ci_recv, k)
     ci_t[...] = ci[...].reshape(coarse, coarse).T

time: 37.9 us -> 37.9 us (level)
  no operation moved by 1% of the time
where the time goes in v4:
time: 37.9 us; the launch traced here: 37.7 us
  Pallas kernels  33.9 us (89%)
  between operations  2.33 us (6%)
  local copies, waits for them, and re-layouts  1.52 us (4%)
    pallas_call x1, Pallas kernels, body(): pl.pallas_call(functools.partial(kernel, cfg), out_shape=(jax.ShapeDtypeS...  33.9 us
    unnamed x1, local copies, waits for them, and re-layouts  1.52 us

profile of v4, /device:TPU:0, one launch (start us, length us, event | category | flops | bytes accessed | tf_op | source)
XLA Modules:
  0.0 37.7 jit_solution(6265032402950230987)
XLA Ops:
  0.6 33.9 %shard_map.95 = (f32[6,4,768]{2,1,0:T(4,128)}, f32[1,1]{1,0:T(1,128)}) custom-call(f32[6,4,768]{2,1,0:T(4,128)} %bitcast.9, f32[6,4,768]{2,1,0:T(4,128)} %bitcast.10, s32[4,4,6]{2,1,0:T(4,128)} %bitcast.11, bf16[4,6,192,768]{3,2,1,0:T(8,128)(2,1)} %inv_hbm.1, bf16[4,6,24,768]{3,2,1,0:T(8,128)(2,1)} %bitcast.7, s32[1,32]{1,0:T(1,128)} %bitcast.12, ...), custom_call_target="tpu_custom_call" | custom-call | tf_op jit(solution)/shard_map/pallas_call | solution.py:440
  34.5 1.5 %copy.12 = f32[4,6,768]{2,0,1:T(4,128)} copy(f32[4,6,768]{2,0,1:T(4,128)} %bitcast.8) | data formatting | bytes 147456
